TPU v7x, 32 devices: a whole 2x2x4 slice. The times are simulated.
32 devices in a mesh: gx: 8 (over y, x, core), gy: 4 (over z).
Axes of the slice: x: 2, y: 2, z: 4, core: 2. Of those that a mesh axis runs over, the one named last changes fastest.
Arguments:
- fields: bfloat16 [2, 64, 16, 32, 128], P(None, None, 'gx', 'gy'), may hold values from -6 to 6
- depth_kernel: bfloat16 [64, 3, 3, 3], replicated, may hold values from -1.25 to 1.25
- point_in: bfloat16 [256, 64], replicated, may hold values from -0.75 to 0.75
- point_out: bfloat16 [64, 256], replicated, may hold values from -0.375 to 0.375
- down_kernel: bfloat16 [128, 64, 2, 2, 2], replicated, may hold values from -0.25 to 0.25
- cotangent: bfloat16 [8, 4, 1, 128, 2, 4, 64], P('gx', 'gy'), may hold values from -6 to 6
Outputs:
- coarse: bfloat16 [8, 4, 1, 128, 2, 4, 64], P('gx', 'gy')
- grad_fields: bfloat16 [2, 64, 16, 32, 128], P(None, None, 'gx', 'gy')
- grad_depth_kernel: float32 [64, 3, 3, 3], replicated
- grad_point_in: float32 [256, 64], replicated
- grad_point_out: float32 [64, 256], replicated
- grad_down_kernel: float32 [128, 64, 2, 2, 2], replicated
All inputs are finite; a program needn't handle non-finite values.
Results may differ from a plain program's by a relative error of at most 0.0066.
Values may be sent and summed in bfloat16 or wider, within the bound.
No kernel may reach another device: no remote copies, remote signals or barrier semaphores. Data moves between devices by JAX's collectives and lax.ppermute only.
A program may use at most 192 MiB of HBM per device.

v0:
```python
import math

import jax
import jax.numpy as jnp
from jax import lax
from jax.sharding import PartitionSpec as P

GRIDC = 4


def padded_2(x, sides, width):
    for axis, dim in sides:
        peers, length = (lax.axis_size(axis), x.shape[dim])
        up = [(i, (i + 1) % peers) for i in range(peers - 1)]
        down = [(j, i) for i, j in up]
        last = lax.slice_in_dim(x, length - width, length, axis=dim)
        initial = lax.slice_in_dim(x, 0, width, axis=dim)
        before = lax.ppermute(last, axis, up)
        after = lax.ppermute(initial, axis, down)
        x = jnp.concatenate([before, x, after], axis=dim)
    return x


def shifted(block, axis, distance):
    devices = range(lax.axis_size(axis))
    route = [((i - distance) % len(devices), i) for i in devices]
    return lax.ppermute(block, axis, route)


def for_sending(x):
    return jax.tree.map(lambda a: a.astype(jnp.bfloat16) if a.dtype == jnp.float32 else a, x)


def gelu_slope(values):
    outputs, pullback = jax.vjp(jax.nn.gelu, values)
    return pullback(jnp.ones_like(outputs))[0]


def depth_conv(padded, weights, span_x, span_y, span_z):
    summed = jnp.zeros(padded.shape[:-3] + (span_x, span_y, span_z), jnp.float32)
    for offset_x in range(3):
        for offset_y in range(3):
            for offset_z in range(3):
                factor = weights[:, offset_x, offset_y, offset_z].astype(jnp.float32)[
                    :, None, None, None
                ]
                window = padded[
                    ...,
                    offset_x : offset_x + span_x,
                    offset_y : offset_y + span_y,
                    offset_z : offset_z + span_z,
                ]
                summed = summed + factor * window
    return summed


def pad_rims(blocks):
    widened = padded_2(blocks, (("gx", 2), ("gy", 3)), 1)
    return jnp.pad(widened, ((0, 0), (0, 0), (0, 0), (0, 0), (1, 1)))


def move_x(part, amount):
    return shifted(part, "gx", amount)


def move_y(part, amount):
    return jax.tree.map(
        lambda part, own: part.astype(own.dtype), shifted(for_sending(part), "gy", amount), part
    )


def regroup(blocks, position, along_x):
    group_size = blocks.shape[0]
    mover = move_x if along_x else move_y
    member = position % group_size
    received = [lax.dynamic_index_in_dim(blocks, member, 0, keepdims=False)]
    for offset in range(1, group_size):
        outgoing = lax.dynamic_index_in_dim(
            blocks, (member + offset) % group_size, 0, keepdims=False
        )
        near_part = mover(outgoing, offset)
        far_part = mover(outgoing, offset - group_size)
        received.append(jnp.where(member >= offset, near_part, far_part))
    stacked = jnp.stack(received)
    reorder = (member - jnp.arange(group_size, dtype=jnp.int32)) % group_size
    return jnp.take(stacked, reorder, axis=0)


def per_device(fields, depth_kernel, point_in, point_out, down_kernel, cotangent):
    samples, chans, span_x, span_y, span_z = fields.shape
    half_x, half_y, half_z = (span_x // 2, span_y // 2, span_z // 2)
    out_chans = down_kernel.shape[0]
    group_x = lax.axis_size("gx") // GRIDC
    group_y = lax.axis_size("gy") // GRIDC
    index_x = lax.axis_index("gx")
    index_y = lax.axis_index("gy")
    padded = pad_rims(fields)
    depth_out = depth_conv(padded, depth_kernel, span_x, span_y, span_z).astype(jnp.bfloat16)
    flat_depth = depth_out.reshape(samples, chans, -1)
    flat_fields = fields.reshape(samples, chans, -1)

    def forward_one(inputs):
        depth_one, field_one = inputs
        preact = jnp.dot(point_in, depth_one, preferred_element_type=jnp.float32)
        active = jax.nn.gelu(preact).astype(jnp.bfloat16)
        branch = jnp.dot(point_out, active, preferred_element_type=jnp.float32)
        return (field_one.astype(jnp.float32) + branch).astype(jnp.bfloat16)

    merged = lax.map(forward_one, (flat_depth, flat_fields))
    patches = (
        merged.reshape(samples, chans, half_x, 2, half_y, 2, half_z, 2)
        .transpose(0, 1, 3, 5, 7, 2, 4, 6)
        .reshape(samples, chans * 8, -1)
    )
    down_mat = down_kernel.reshape(out_chans, chans * 8)
    reduced = jnp.einsum(
        "ok,skn->son", down_mat, patches, preferred_element_type=jnp.float32
    ).astype(jnp.bfloat16)
    reduced = reduced.reshape(samples, out_chans, half_x, half_y, half_z)
    sectioned = regroup(
        reduced.reshape(group_x, samples // group_x, out_chans, half_x, half_y, half_z),
        index_x,
        True,
    )
    wide_x = group_x * half_x
    sectioned = sectioned.transpose(1, 2, 0, 3, 4, 5).reshape(
        samples // group_x, out_chans, wide_x, half_y, half_z
    )
    per_group = samples // (group_x * group_y)
    sectioned = regroup(
        sectioned.reshape(group_y, per_group, out_chans, wide_x, half_y, half_z), index_y, False
    )
    coarse = sectioned.transpose(1, 2, 3, 0, 4, 5).reshape(
        per_group, out_chans, wide_x, group_y * half_y, half_z
    )[None, None]
    incoming = (
        cotangent[0, 0]
        .reshape(per_group, out_chans, wide_x, group_y, half_y, half_z)
        .transpose(3, 0, 1, 2, 4, 5)
    )
    incoming = regroup(incoming, index_y, False).reshape(
        group_y * per_group, out_chans, wide_x, half_y, half_z
    )
    incoming = incoming.reshape(
        group_y * per_group, out_chans, group_x, half_x, half_y, half_z
    ).transpose(2, 0, 1, 3, 4, 5)
    grad_down = regroup(incoming, index_x, True).reshape(samples, out_chans, -1)
    grad_patch = jnp.einsum("ok,son->skn", down_mat, grad_down, preferred_element_type=jnp.float32)
    grad_merged = (
        grad_patch.reshape(samples, chans, 2, 2, 2, half_x, half_y, half_z)
        .transpose(0, 1, 5, 2, 6, 3, 7, 4)
        .reshape(samples, chans, -1)
        .astype(jnp.bfloat16)
    )
    grad_downw = jnp.einsum("son,skn->ok", grad_down, patches, preferred_element_type=jnp.float32)

    def backward_one(inputs):
        depth_one, merged_grad = inputs
        preact = jnp.dot(point_in, depth_one, preferred_element_type=jnp.float32)
        active = jax.nn.gelu(preact).astype(jnp.bfloat16)
        grad_active = jnp.dot(point_out.T, merged_grad, preferred_element_type=jnp.float32)
        grad_pre = (grad_active * gelu_slope(preact)).astype(jnp.bfloat16)
        outw = jnp.dot(merged_grad, active.T, preferred_element_type=jnp.float32)
        inw = jnp.dot(grad_pre, depth_one.T, preferred_element_type=jnp.float32)
        depth_grad = jnp.dot(point_in.T, grad_pre, preferred_element_type=jnp.float32).astype(
            jnp.bfloat16
        )
        return (depth_grad, outw, inw)

    grad_depth, outw_parts, inw_parts = lax.map(backward_one, (flat_depth, grad_merged))
    grad_outw = jnp.sum(outw_parts, axis=0)
    grad_inw = jnp.sum(inw_parts, axis=0)
    grad_depth = grad_depth.reshape(fields.shape)
    grad_pad = pad_rims(grad_depth)
    adjoint = depth_conv(grad_pad, depth_kernel[:, ::-1, ::-1, ::-1], span_x, span_y, span_z)
    grad_fields = (grad_merged.reshape(fields.shape).astype(jnp.float32) + adjoint).astype(
        jnp.bfloat16
    )
    columns = []
    for offset_x in range(3):
        for offset_y in range(3):
            for offset_z in range(3):
                window = padded[
                    :,
                    :,
                    offset_x : offset_x + span_x,
                    offset_y : offset_y + span_y,
                    offset_z : offset_z + span_z,
                ]
                columns.append(
                    lax.dot_general(
                        grad_depth,
                        window,
                        (((0, 2, 3, 4), (0, 2, 3, 4)), ((1,), (1,))),
                        preferred_element_type=jnp.float32,
                    )
                )
    grad_depthw = jnp.stack(columns, axis=1).reshape(chans, 3, 3, 3)
    totals = lax.psum(
        (grad_depthw, grad_inw, grad_outw, grad_downw.reshape(out_chans, chans, 2, 2, 2)),
        ("gx", "gy"),
    )
    norm_scale = 1.0 / math.sqrt(
        samples * span_x * span_y * span_z * lax.axis_size("gx") * lax.axis_size("gy")
    )
    return (
        coarse,
        grad_fields,
        totals[0] * norm_scale,
        totals[1] * norm_scale,
        totals[2] * norm_scale,
        totals[3] * norm_scale,
    )


def solution(mesh):
    placed = (
        P(None, None, "gx", "gy", None),
        P(),
        P(),
        P(),
        P(),
        P("gx", "gy", None, None, None, None, None),
    )
    return jax.shard_map(
        per_device,
        mesh=mesh,
        in_specs=placed,
        out_specs=(
            P("gx", "gy", None, None, None, None, None),
            P(None, None, "gx", "gy", None),
            P(),
            P(),
            P(),
            P(),
        ),
        check_vma=False,
    )
```

profile of v0, /device:TPU:0, one launch (start us, length us, event | category | flops | bytes accessed | tf_op | source)
XLA Modules:
  0.0 365.5 jit_solution(18013525221591987385)
XLA Ops:
  7.3 1.5 dynamic-slice_bitcast_fusion
  8.8 3.3 collective-permute-start.7
  12.1 1.6 copy.43
  14.7 1.3 collective-permute-start.1
  16.0 3.1 collective-permute-start
  20.2 1.0 reshape.305
  21.6 3.5 collective-permute-start.2
  25.1 1.3 collective-permute-start.3
  26.5 2.5 collective-permute-done.2
  29.0 4.4 %collective-permute-done.3 = bf16[2,64,4,1,128]{1,4,3,2,0:T(8,128)(2,1)S(1)} collective-permute-done((bf16[2,64,4,1,128]{1,4,3,2,0:T(8,128)(2,1)S(1)}, bf16[2,64,4,1,128]{1,4,3,2,0:T(8,128)(2,1)S(1)}, u32[]{:S(2)}, u32[]{:S(2)}) %collective-permute-start.3) | collective-permute-done | bytes 131104 | tf_op jit(solution)/shard_map/ppermute | solution.py:19
  33.4 2.5 select_maximum_fusion.4
  36.0 1.3 maximum_maximum_fusion
  37.6 8.9 %add_convert_fusion.1 = bf16[2,64,2,8,128]{1,4,3,2,0:T(8,128)(2,1)} fusion(bf16[2,64,2,8,128]{1,4,3,2,0:T(8,128)(2,1)S(1)} %copy-done.4, f32[64]{0:T(128)S(1)} %copy-done.32, f32[64]{0:T(128)S(1)} %copy-done.34, f32[64]{0:T(128)S(1)} %get-tuple-element.273, f32[64]{0:T(128)S(1)} %get-tuple-element.274, f32[64]{0:T(128)S(1)} %get-tuple-element.275, ...), kind=kLoop, calls=%fused_computation.135 | loop fusion | flops 21757952 | bytes 14162688 | tf_op jit(solution)/shard_map/convert_element_type | solution.py:98
  46.5 1.6 copy.49
  48.9 5.7 %while.26 = (s32[]{:T(128)}, bf16[2,64,2048]{2,1,0:T(8,128)(2,1)}, bf16[2,64,2048]{2,1,0:T(8,128)(2,1)}, bf16[2,64,2048]{2,1,0:T(8,128)(2,1)S(1)}, bf16[256,64]{...) while((s32[]{:T(128)}, bf16[2,64,2048]{2,1,0:T(8,128)(2,1)}, bf16[2,64,2048]{2,1,0:T(8,128)(2,1)}, ...), condition=%wide.region_1.2_spmd, body=%wide.region_0.1_spmd.sunk | while | flops 139329536 | bytes 853077 | solution.py:109
  48.9 2.8 fusion.125
  51.7 2.8 fusion.125
  54.6 2.4 copy.50
  56.9 3.9 %copy.51 = bf16[2,64,2,2,2,1,4,64]{7,6,4,3,2,1,0,5:T(4,128)(2,1)} copy(bf16[2,64,2,2,2,1,4,64]{1,4,7,3,6,2,0,5:T(2,128)(2,1)} %bitcast.429) | data formatting | bytes 1048576 | tf_op jit(solution)/shard_map/transpose | solution.py:112
  60.8 2.7 reshape.308
  63.6 1.4 convolution_convert_fusion.2
  65.7 3.4 collective-permute-start.4
  69.0 1.5 maximum_bitcast_fusion.1
  70.5 2.1 gather_fusion.1
  72.7 2.4 copy.62
  75.0 6.2 %collective-permute-done.4 = bf16[1,128,1,4,64]{1,4,3,2,0:T(8,128)(2,1)} collective-permute-done((bf16[1,128,1,4,64]{1,4,3,2,0:T(8,128)(2,1)}, bf16[1,128,1,4,64]{1,4,3,2,0:T(8,128)(2,1)}, u32[]{:S(2)}, u32[]{:S(2)}) %collective-permute-start.4) | collective-permute-done | bytes 65568 | tf_op jit(solution)/shard_map/ppermute | solution.py:27
  82.1 1.5 maximum_bitcast_fusion
  83.6 2.1 gather_fusion
  85.7 1.7 bitcast_select_fusion
  88.1 1.1 fusion.86
  89.2 2.1 copy.55
  91.3 2.8 convert_element_type.648
  94.0 3.5 copy_bitcast_fusion
  97.5 3.7 %copy.58 = bf16[2,64,1,2,4,2,64,2]{1,7,6,5,4,3,0,2:T(2,128)(2,1)} copy(bf16[2,64,1,2,4,2,64,2]{6,1,7,5,4,3,2,0:T(8,128)(2,1)} %get-tuple-element.264) | data formatting | bytes 1048576 | tf_op jit(solution)/shard_map/convert_element_type | solution.py:176
  101.2 2.4 copy.59
  104.4 10.3 %while.27 = (s32[]{:T(128)}, bf16[2,64,2048]{2,1,0:T(8,128)(2,1)}, f32[2,64,256]{2,1,0:T(8,128)}, f32[2,256,64]{1,2,0:T(8,128)}, bf16[2,64,2048]{2,1,0:T(8,128)(...) while((s32[]{:T(128)}, bf16[2,64,2048]{2,1,0:T(8,128)(2,1)}, ...), condition=%wide.region_3.5_spmd, body=%wide.region_2.4_spmd.sunk | while | flops 350355456 | bytes 19368244 | solution.py:170
  106.3 1.5 fusion.135
  111.5 1.5 fusion.135
  114.8 1.5 reduce_sum.18
  116.3 1.5 reduce_sum.19
  117.9 2.3 copy.61
  120.2 3.0 bitcast_convert_fusion.27
  123.2 7.4 %fusion.85 = (f32[64]{0:T(128)S(1)}, f32[64]{0:T(128)S(1)}, f32[64]{0:T(128)S(1)}, f32[64]{0:T(128)S(1)}, f32[64]{0:T(128)S(1)}, /*index=5*/f32[64]{0:T(128)S(1)...) fusion(bf16[64,2,2,8,128]{0,4,3,2,1:T(8,128)(2,1)S(1)} %bitcast, ...), kind=kLoop, calls=%fused_computation.133 | loop fusion | flops 14416768 | bytes 9966080 | tf_op jit(solution)/shard_map/dot_general | solution.py:191
  130.6 1.1 fusion.91
  131.7 2.1 collective-permute-start.8
  133.8 1.6 collective-permute-start.9
  135.3 3.2 copy.153
  138.5 1.9 multiply_reduce_fusion
  140.5 4.3 %fusion.84 = (f32[64]{0:T(128)S(1)}, f32[64]{0:T(128)S(1)}, f32[64]{0:T(128)S(1)}, f32[64]{0:T(128)S(1)}, f32[64]{0:T(128)S(1)}, /*index=5*/f32[64]{0:T(128)S(1)}, f32[64]{0:T(128)S(1)}, f32[64]{0:T(128)S(1)}) fusion(bf16[64,2,2,8,128]{0,4,3,2,1:T(8,128)(2,1)S(1)} %bitcast.422, bf16[2,64,4,9,128]{1,4,3,2,0:T(8,128)(2,1)} %copy-done.7, ...), kind=kLoop, calls=%fused_computation.132 | loop fusion | flops 7077376 | bytes 4720640 | tf_op jit(solution)/shard_map/dot_general | solution.py:191
  144.9 44.5 %psum.28 = f32[64,3,3,3]{0,3,2,1:T(4,128)S(1)} all-reduce(f32[64,3,3,3]{0,3,2,1:T(4,128)S(1)} %reshape.312), channel_id=1, replica_groups=mesh['gx'=8,'gy'=4] {'gx','gy'}, use_global_device_ids=true, to_apply=%region_4.6 | all-reduce | flops 1728 | bytes 13824 | tf_op jit(solution)/shard_map/psum | solution.py:199
  189.3 3.0 copy.57
  192.3 2.1 convolution_bitcast_fusion.6
  195.0 129.5 %all-reduce.5.cloned.1.call-done = (f32[256,64]{0,1:T(8,128)}, f32[64,256]{1,0:T(8,128)}, f32[128,64,2,2,2]{0,1,4,3,2:T(8,128)}) async-done(((f32[256,64]{0,1:T(8,128)}, f32[64,256]{1,0:T(8,128)}, f32[128,64,2,2,2]{0,1,4,3,2:T(8,128)}), (f32[256,64]{0,1:T(8,128)}, f32[64,256]{1,0:T(8,128)}, f32[128,64,2,2,2]{0,1,4,3,2:T(8,128)})) %all-reduce.5.cloned.1.call-update) | async-done | bytes 393232 | tf_op jit(solution)/shard_map/psum | solution.py:199
  324.5 1.0 broadcast_multiply_fusion
  326.4 1.5 broadcast_multiply_fusion.2
  327.9 1.1 pad_maximum_fusion.8
  329.0 3.3 collective-permute-start.10
  332.2 1.3 collective-permute-start.11
  334.2 2.1 collective-permute-done.10
  336.2 4.3 %collective-permute-done.11 = bf16[2,64,4,1,128]{1,4,3,2,0:T(8,128)(2,1)S(1)} collective-permute-done((bf16[2,64,4,1,128]{1,4,3,2,0:T(8,128)(2,1)S(1)}, bf16[2,64,4,1,128]{1,4,3,2,0:T(8,128)(2,1)S(1)}, u32[]{:S(2)}, u32[]{:S(2)}) %collective-permute-start.11) | collective-permute-done | bytes 131104 | tf_op jit(solution)/shard_map/ppermute | solution.py:19
  340.5 2.3 select_maximum_fusion
  343.1 2.8 maximum_maximum_fusion.1
  346.1 10.1 %add_convert_fusion = bf16[2,64,2,8,128]{1,4,3,2,0:T(8,128)(2,1)} fusion(f32[2,64,2,8,128]{1,4,3,2,0:T(8,128)S(1)} %bitcast.427, bf16[2,64,2,8,128]{1,4,3,2,0:T(8,128)(2,1)S(1)} %bitcast.426, bf16[2,64,4,10,130]{1,4,3,2,0:T(8,128)(2,1)S(1)} %select_maximum_fusion, bf16[2,64,4,9,128]{1,4,3,2,0:T(8,128)(2,1)S(1)} %get-tuple-element.255, ...), kind=kLoop, calls=%fused_computation.134 | loop fusion | flops 22020096 | bytes 15211264 | tf_op jit(solution)/shard_map/convert_element_type | solution.py:176
  356.2 2.5 copy.65
  (202 shorter events, 15.9 us)
Async XLA Ops:
  7.2 56.4 %copy-start = (bf16[128,64,2,2,2]{0,4,3,2,1:T(2,128)(2,1)S(1)}, bf16[128,64,2,2,2]{0,4,3,2,1:T(2,128)(2,1)}, u32[]{:S(2)}) copy-start(bf16[128,64,2,2,2]{0,4,3,2,1:T(2,128)(2,1)} %param.16) | copy-start | bytes 393220
  7.2 13.0 %copy-start.13 = (bf16[2,64,2,8,128]{4,3,2,1,0:T(8,128)(2,1)S(1)}, bf16[2,64,2,8,128]{4,3,2,1,0:T(8,128)(2,1)}, u32[]{:S(2)}) copy-start(bf16[2,64,2,8,128]{4,3,2,1,0:T(8,128)(2,1)} %param.12) | copy-start | bytes 1572868
  7.2 11.9 %copy-start.25 = (bf16[64,3,3,3]{0,3,2,1:T(4,128)(2,1)S(1)}, bf16[64,3,3,3]{0,3,2,1:T(4,128)(2,1)}, u32[]{:S(2)}) copy-start(bf16[64,3,3,3]{0,3,2,1:T(4,128)(2,1)} %param.13) | copy-start | bytes 10372
  7.2 317.3 %all-reduce.5.cloned.1.call-start = ((), (), s32[]{:S(2)}) async-start(), calls=%async_computation | async-start | bytes 786432 | tf_op jit(solution)/shard_map/psum | solution.py:199
  8.8 17.6 %collective-permute-start.7 = (bf16[1,128,1,4,64]{1,4,3,2,0:T(8,128)(2,1)S(1)}, bf16[1,128,1,4,64]{1,4,3,2,0:T(8,128)(2,1)S(1)}, u32[]{:S(2)}, u32[]{:S(2)}) collective-permute-start(bf16[1,128,1,4,64]{1,4,3,2,0:T(8,128)(2,1)S(1)} %get-tuple-element.269), channel_id=1, source_target_pairs={{4,0},{8,4},{12,8},{16,12},{20,16},{24,20},{28,24},{0,28},{5,1},{9... | collective-permute-start | bytes 196616 | tf_op jit(solution)/shard_map/ppermute | solution.py:27
  12.1 14.3 %collective-permute-start.6 = (bf16[1,128,1,4,64]{1,4,3,2,0:T(8,128)(2,1)S(1)}, bf16[1,128,1,4,64]{1,4,3,2,0:T(8,128)(2,1)S(1)}, u32[]{:S(2)}, u32[]{:S(2)}) collective-permute-start(bf16[1,128,1,4,64]{1,4,3,2,0:T(8,128)(2,1)S(1)} %get-tuple-element.269), channel_id=1, source_target_pairs={{28,0},{0,4},{4,8},{8,12},{12,16},{16,20},{20,24},{24,28},{29,1},{... | collective-permute-start | bytes 196616 | tf_op jit(solution)/shard_map/ppermute | solution.py:27
  13.7 7.9 %copy-start.3 = (bf16[2,64,2,8,128]{1,4,3,2,0:T(8,128)(2,1)}, bf16[2,64,2,8,128]{1,4,3,2,0:T(8,128)(2,1)S(1)}, u32[]{:S(2)}) copy-start(bf16[2,64,2,8,128]{1,4,3,2,0:T(8,128)(2,1)S(1)} %copy.43) | copy-start | bytes 1572868
  14.7 6.7 %collective-permute-start.1 = (bf16[2,64,1,8,128]{1,4,3,2,0:T(8,128)(2,1)}, bf16[2,64,1,8,128]{1,4,3,2,0:T(8,128)(2,1)S(1)}, u32[]{:S(2)}, u32[]{:S(2)}) collective-permute-start(bf16[2,64,1,8,128]{1,4,3,2,0:T(8,128)(2,1)} %get-tuple-element.266), channel_id=1, source_target_pairs={{4,0},{8,4},{12,8},{16,12},{20,16},{24,20},{28,24},{5,1},{9,5},{13... | collective-permute-start | bytes 786440 | tf_op jit(solution)/shard_map/ppermute | solution.py:19
  16.0 5.5 %collective-permute-start = (bf16[2,64,1,8,128]{1,4,3,2,0:T(8,128)(2,1)S(1)}, bf16[2,64,1,8,128]{1,4,3,2,0:T(8,128)(2,1)S(1)}, u32[]{:S(2)}, u32[]{:S(2)}) collective-permute-start(bf16[2,64,1,8,128]{1,4,3,2,0:T(8,128)(2,1)S(1)} %get-tuple-element.267), channel_id=1, source_target_pairs={{0,4},{4,8},{8,12},{12,16},{16,20},{20,24},{24,28},{1,5},{5,9},{9,... | collective-permute-start | bytes 786440 | tf_op jit(solution)/shard_map/ppermute | solution.py:18
  21.3 16.0 %copy-start.36 = (f32[64]{0:T(128)}, f32[64]{0:T(128)S(1)}, u32[]{:S(2)}) copy-start(f32[64]{0:T(128)S(1)} %get-tuple-element.272) | copy-start | bytes 772
  21.3 16.0 %copy-start.38 = (f32[64]{0:T(128)}, f32[64]{0:T(128)S(1)}, u32[]{:S(2)}) copy-start(f32[64]{0:T(128)S(1)} %get-tuple-element.273) | copy-start | bytes 772
  21.3 16.0 %copy-start.40 = (f32[64]{0:T(128)}, f32[64]{0:T(128)S(1)}, u32[]{:S(2)}) copy-start(f32[64]{0:T(128)S(1)} %get-tuple-element.274) | copy-start | bytes 772
  21.3 16.0 %copy-start.42 = (f32[64]{0:T(128)}, f32[64]{0:T(128)S(1)}, u32[]{:S(2)}) copy-start(f32[64]{0:T(128)S(1)} %get-tuple-element.275) | copy-start | bytes 772
  21.3 16.0 %copy-start.44 = (f32[64]{0:T(128)}, f32[64]{0:T(128)S(1)}, u32[]{:S(2)}) copy-start(f32[64]{0:T(128)S(1)} %get-tuple-element.276) | copy-start | bytes 772
  21.3 16.0 %copy-start.46 = (f32[64]{0:T(128)}, f32[64]{0:T(128)S(1)}, u32[]{:S(2)}) copy-start(f32[64]{0:T(128)S(1)} %get-tuple-element.277) | copy-start | bytes 772
  21.3 16.0 %copy-start.48 = (f32[64]{0:T(128)}, f32[64]{0:T(128)S(1)}, u32[]{:S(2)}) copy-start(f32[64]{0:T(128)S(1)} %get-tuple-element.278) | copy-start | bytes 772
  21.3 16.0 %copy-start.50 = (f32[64]{0:T(128)}, f32[64]{0:T(128)S(1)}, u32[]{:S(2)}) copy-start(f32[64]{0:T(128)S(1)} %get-tuple-element.279) | copy-start | bytes 772
  21.3 16.0 %copy-start.52 = (f32[64]{0:T(128)}, f32[64]{0:T(128)S(1)}, u32[]{:S(2)}) copy-start(f32[64]{0:T(128)S(1)} %get-tuple-element.280) | copy-start | bytes 772
  21.4 16.0 %copy-start.54 = (f32[64]{0:T(128)}, f32[64]{0:T(128)S(1)}, u32[]{:S(2)}) copy-start(f32[64]{0:T(128)S(1)} %get-tuple-element.281) | copy-start | bytes 772
  21.4 16.0 %copy-start.56 = (f32[64]{0:T(128)}, f32[64]{0:T(128)S(1)}, u32[]{:S(2)}) copy-start(f32[64]{0:T(128)S(1)} %get-tuple-element.282) | copy-start | bytes 772
  21.4 16.0 %copy-start.58 = (f32[64]{0:T(128)}, f32[64]{0:T(128)S(1)}, u32[]{:S(2)}) copy-start(f32[64]{0:T(128)S(1)} %get-tuple-element.283) | copy-start | bytes 772
  21.4 16.0 %copy-start.60 = (f32[64]{0:T(128)}, f32[64]{0:T(128)S(1)}, u32[]{:S(2)}) copy-start(f32[64]{0:T(128)S(1)} %get-tuple-element.284) | copy-start | bytes 772
  21.4 16.0 %copy-start.62 = (f32[64]{0:T(128)}, f32[64]{0:T(128)S(1)}, u32[]{:S(2)}) copy-start(f32[64]{0:T(128)S(1)} %get-tuple-element.285) | copy-start | bytes 772
  21.4 16.0 %copy-start.64 = (f32[64]{0:T(128)}, f32[64]{0:T(128)S(1)}, u32[]{:S(2)}) copy-start(f32[64]{0:T(128)S(1)} %get-tuple-element.286) | copy-start | bytes 772
  21.4 16.0 %copy-start.66 = (f32[64]{0:T(128)}, f32[64]{0:T(128)S(1)}, u32[]{:S(2)}) copy-start(f32[64]{0:T(128)S(1)} %get-tuple-element.287) | copy-start | bytes 772
  21.4 16.0 %copy-start.68 = (f32[64]{0:T(128)}, f32[64]{0:T(128)S(1)}, u32[]{:S(2)}) copy-start(f32[64]{0:T(128)S(1)} %get-tuple-element.288) | copy-start | bytes 772
  21.4 16.0 %copy-start.70 = (f32[64]{0:T(128)}, f32[64]{0:T(128)S(1)}, u32[]{:S(2)}) copy-start(f32[64]{0:T(128)S(1)} %get-tuple-element.289) | copy-start | bytes 772
  21.4 16.0 %copy-start.72 = (f32[64]{0:T(128)}, f32[64]{0:T(128)S(1)}, u32[]{:S(2)}) copy-start(f32[64]{0:T(128)S(1)} %get-tuple-element.290) | copy-start | bytes 772
  21.5 16.0 %copy-start.8 = (bf16[2,64,1,8,128]{1,4,3,2,0:T(8,128)(2,1)}, bf16[2,64,1,8,128]{1,4,3,2,0:T(8,128)(2,1)S(1)}, u32[]{:S(2)}) copy-start(bf16[2,64,1,8,128]{1,4,3,2,0:T(8,128)(2,1)S(1)} %collective-permute-done.1) | copy-start | bytes 786436
  21.5 7.5 %copy-start.10 = (bf16[2,64,1,8,128]{1,4,3,2,0:T(8,128)(2,1)}, bf16[2,64,1,8,128]{1,4,3,2,0:T(8,128)(2,1)S(1)}, u32[]{:S(2)}) copy-start(bf16[2,64,1,8,128]{1,4,3,2,0:T(8,128)(2,1)S(1)} %collective-permute-done) | copy-start | bytes 786436
  21.6 7.4 %collective-permute-start.2 = (bf16[2,64,4,1,128]{1,4,3,2,0:T(8,128)(2,1)S(1)}, bf16[2,64,4,1,128]{1,4,3,2,0:T(8,128)(2,1)S(1)}, u32[]{:S(2)}, u32[]{:S(2)}) collective-permute-start(bf16[2,64,4,1,128]{1,4,3,2,0:T(8,128)(2,1)S(1)} %get-tuple-element.260), channel_id=1, source_target_pairs={{0,1},{1,2},{2,3},{4,5},{5,6},{6,7},{8,9},{9,10},{10,11},{12,13},{... | collective-permute-start | bytes 393224 | tf_op jit(solution)/shard_map/ppermute | solution.py:18
  25.1 8.3 %collective-permute-start.3 = (bf16[2,64,4,1,128]{1,4,3,2,0:T(8,128)(2,1)S(1)}, bf16[2,64,4,1,128]{1,4,3,2,0:T(8,128)(2,1)S(1)}, u32[]{:S(2)}, u32[]{:S(2)}) collective-permute-start(bf16[2,64,4,1,128]{1,4,3,2,0:T(8,128)(2,1)S(1)} %get-tuple-element.261), channel_id=1, source_target_pairs={{1,0},{2,1},{3,2},{5,4},{6,5},{7,6},{9,8},{10,9},{11,10},{13,12},{... | collective-permute-start | bytes 393224 | tf_op jit(solution)/shard_map/ppermute | solution.py:19
  26.5 9.4 %copy-start.4 = (bf16[2,64,2,8,128]{1,4,3,2,0:T(8,128)(2,1)S(1)}, bf16[2,64,2,8,128]{1,4,3,2,0:T(8,128)(2,1)}, u32[]{:S(2)}) copy-start(bf16[2,64,2,8,128]{1,4,3,2,0:T(8,128)(2,1)} %copy-done.3) | copy-start | bytes 1572868
  37.3 9.2 %copy-start.6 = (bf16[2,64,4,9,128]{1,4,3,2,0:T(8,128)(2,1)}, bf16[2,64,4,9,128]{1,4,3,2,0:T(8,128)(2,1)S(1)}, u32[]{:S(2)}) copy-start(bf16[2,64,4,9,128]{1,4,3,2,0:T(8,128)(2,1)S(1)} %get-tuple-element.258) | copy-start | bytes 3538948
  37.3 9.2 %copy-start.7 = (bf16[2,64,4,9,128]{1,4,3,2,0:T(8,128)(2,1)}, bf16[2,64,4,9,128]{1,4,3,2,0:T(8,128)(2,1)S(1)}, u32[]{:S(2)}) copy-start(bf16[2,64,4,9,128]{1,4,3,2,0:T(8,128)(2,1)S(1)} %get-tuple-element.259) | copy-start | bytes 3538948
  65.7 9.4 %collective-permute-start.5 = (bf16[1,128,1,4,64]{1,4,3,2,0:T(8,128)(2,1)}, bf16[1,128,1,4,64]{1,4,3,2,0:T(8,128)(2,1)}, u32[]{:S(2)}, u32[]{:S(2)}) collective-permute-start(bf16[1,128,1,4,64]{1,4,3,2,0:T(8,128)(2,1)} %get-tuple-element.271), channel_id=1, source_target_pairs={{4,0},{8,4},{12,8},{16,12},{20,16},{24,20},{28,24},{0,28},{5,1},{9... | collective-permute-start | bytes 196616 | tf_op jit(solution)/shard_map/ppermute | solution.py:27
  65.7 15.6 %collective-permute-start.4 = (bf16[1,128,1,4,64]{1,4,3,2,0:T(8,128)(2,1)}, bf16[1,128,1,4,64]{1,4,3,2,0:T(8,128)(2,1)}, u32[]{:S(2)}, u32[]{:S(2)}) collective-permute-start(bf16[1,128,1,4,64]{1,4,3,2,0:T(8,128)(2,1)} %get-tuple-element.271), channel_id=1, source_target_pairs={{28,0},{0,4},{4,8},{8,12},{12,16},{16,20},{20,24},{24,28},{29,1},{... | collective-permute-start | bytes 196616 | tf_op jit(solution)/shard_map/ppermute | solution.py:27
  97.5 6.9 %copy-start.74 = (bf16[64,256]{1,0:T(8,128)(2,1)S(1)}, bf16[64,256]{1,0:T(8,128)(2,1)}, u32[]{:S(2)}) copy-start(bf16[64,256]{1,0:T(8,128)(2,1)} %get-tuple-element.466) | copy-start | bytes 98308
  131.7 196.2 %collective-permute-start.8 = (bf16[2,64,1,8,128]{1,4,3,2,0:T(8,128)(2,1)}, bf16[2,64,1,8,128]{1,4,3,2,0:T(8,128)(2,1)}, u32[]{:S(2)}, u32[]{:S(2)}) collective-permute-start(bf16[2,64,1,8,128]{1,4,3,2,0:T(8,128)(2,1)} %get-tuple-element.262), channel_id=1, source_target_pairs={{0,4},{4,8},{8,12},{12,16},{16,20},{20,24},{24,28},{1,5},{5,9},{9,... | collective-permute-start | bytes 786440 | tf_op jit(solution)/shard_map/ppermute | solution.py:18
  133.8 6.7 %copy-start.2 = (bf16[2,64,2048]{1,2,0:T(8,128)(2,1)S(1)}, bf16[2,64,2048]{1,2,0:T(8,128)(2,1)}, u32[]{:S(2)}) copy-start(bf16[2,64,2048]{1,2,0:T(8,128)(2,1)} %copy.61) | copy-start | bytes 1572868
  133.8 6.7 %copy-start.5 = (bf16[2,64,2,8,128]{1,4,3,2,0:T(8,128)(2,1)S(1)}, bf16[2,64,2,8,128]{1,4,3,2,0:T(8,128)(2,1)}, u32[]{:S(2)}) copy-start(bf16[2,64,2,8,128]{1,4,3,2,0:T(8,128)(2,1)} %copy-done.3) | copy-start | bytes 1572868
  133.8 6.7 %copy-start.9 = (bf16[2,64,1,8,128]{1,4,3,2,0:T(8,128)(2,1)S(1)}, bf16[2,64,1,8,128]{1,4,3,2,0:T(8,128)(2,1)}, u32[]{:S(2)}) copy-start(bf16[2,64,1,8,128]{1,4,3,2,0:T(8,128)(2,1)} %copy-done.8) | copy-start | bytes 786436
  133.8 6.7 %copy-start.12 = (bf16[2,64,1,8,128]{1,4,3,2,0:T(8,128)(2,1)S(1)}, bf16[2,64,1,8,128]{1,4,3,2,0:T(8,128)(2,1)}, u32[]{:S(2)}) copy-start(bf16[2,64,1,8,128]{1,4,3,2,0:T(8,128)(2,1)} %copy-done.10) | copy-start | bytes 786436
  133.8 194.1 %collective-permute-start.9 = (bf16[2,64,1,8,128]{1,4,3,2,0:T(8,128)(2,1)}, bf16[2,64,1,8,128]{1,4,3,2,0:T(8,128)(2,1)}, u32[]{:S(2)}, u32[]{:S(2)}) collective-permute-start(bf16[2,64,1,8,128]{1,4,3,2,0:T(8,128)(2,1)} %get-tuple-element.263), channel_id=1, source_target_pairs={{4,0},{8,4},{12,8},{16,12},{20,16},{24,20},{28,24},{5,1},{9,5},{13... | collective-permute-start | bytes 786440 | tf_op jit(solution)/shard_map/ppermute | solution.py:19
  324.5 9.0 %copy-start.24 = (f32[64,256]{1,0:T(8,128)S(1)}, f32[64,256]{1,0:T(8,128)}, u32[]{:S(2)}) copy-start(f32[64,256]{1,0:T(8,128)} %get-tuple-element.252) | copy-start | bytes 196612
  329.0 7.3 %collective-permute-start.10 = (bf16[2,64,4,1,128]{1,4,3,2,0:T(8,128)(2,1)S(1)}, bf16[2,64,4,1,128]{1,4,3,2,0:T(8,128)(2,1)S(1)}, u32[]{:S(2)}, u32[]{:S(2)}) collective-permute-start(bf16[2,64,4,1,128]{1,4,3,2,0:T(8,128)(2,1)S(1)} %get-tuple-element.256), channel_id=1, source_target_pairs={{0,1},{1,2},{2,3},{4,5},{5,6},{6,7},{8,9},{9,10},{10,11},{12,13},{... | collective-permute-start | bytes 393224 | tf_op jit(solution)/shard_map/ppermute | solution.py:18
  332.2 8.3 %collective-permute-start.11 = (bf16[2,64,4,1,128]{1,4,3,2,0:T(8,128)(2,1)S(1)}, bf16[2,64,4,1,128]{1,4,3,2,0:T(8,128)(2,1)S(1)}, u32[]{:S(2)}, u32[]{:S(2)}) collective-permute-start(bf16[2,64,4,1,128]{1,4,3,2,0:T(8,128)(2,1)S(1)} %get-tuple-element.257), channel_id=1, source_target_pairs={{1,0},{2,1},{3,2},{5,4},{6,5},{7,6},{9,8},{10,9},{11,10},{13,12},{... | collective-permute-start | bytes 393224 | tf_op jit(solution)/shard_map/ppermute | solution.py:19
  342.9 3.0 copy-start.27
  342.9 3.0 copy-start.29
  342.9 3.0 copy-start.31
  342.9 3.0 copy-start.33
  342.9 3.0 copy-start.35
  342.9 3.0 copy-start.37
  342.9 3.0 copy-start.39
  342.9 3.0 copy-start.41
  342.9 3.0 copy-start.43
  342.9 3.0 copy-start.45
  343.0 3.0 copy-start.47
  343.0 3.0 copy-start.49
  343.0 3.0 copy-start.51
  343.0 3.0 copy-start.53
  343.0 3.0 copy-start.55
  343.0 3.0 copy-start.57
  343.0 3.0 copy-start.59
  (31 other events, 57.7 us)
Sparse Core Ops, SparseCore 0:
  194.5 129.9 all-reduce.4
where the time goes:
time: 367 us; the launch traced here: 366 us
  waiting for transfers between devices  149 us (41%)
  other arithmetic  62.7 us (17%)
  local copies, waits for them, and re-layouts  52.8 us (14%)
  blocking collectives  44.5 us (12%)
  starting transfers between devices  24.1 us (7%)
  matrix products  17.2 us (5%)
  between operations  15.2 us (4%)
    psum x1, waiting for transfers between devices, per_device(): lax.psum((grad_depthw, grad_inw, grad_outw, grad_downw.reshape(out_chans,...  129 us
    psum x1, blocking collectives, per_device(): lax.psum((grad_depthw, grad_inw, grad_outw, grad_downw.reshape(out_chans,...  44.5 us
    dot_general x3, other arithmetic, per_device(): lax.dot_general(grad_depth, window, (((0, 2, 3, 4), (0, 2, 3, 4)), ((1,),...  13.6 us
    ppermute x4, starting transfers between devices, padded_2(): before = lax.ppermute(last, axis, up)  11.9 us
    convert_element_type x1, other arithmetic, per_device(): (grad_merged.reshape(fields.shape).astype(jnp.float32) + adjoint).astype(...  10.1 us
    convert_element_type x3, local copies, waits for them, and re-layouts, per_device(): grad_merged.reshape(fields.shape).astype(jnp.float32) + adjoint  9.38 us
    unnamed x140, local copies, waits for them, and re-layouts  9.07 us
    concatenate x4, other arithmetic, padded_2(): x = jnp.concatenate([before, x, after], axis=dim)  8.93 us
  transfers between devices with their start and end apart: 13, of which 6 were waited for; matrix products, arithmetic and copies ran while one was open for 8% of the time, Pallas kernels for 0%

commit v1 on v0

v1 whole, which is shorter than its diff:
```python
import functools
import math

import jax
import jax.numpy as jnp
from jax import lax
from jax.experimental import pallas as pl
from jax.experimental.pallas import tpu as pltpu
from jax.sharding import PartitionSpec as P

GRIDC = 4
F32 = jnp.float32
BF16 = jnp.bfloat16
VMEM_LIMIT = 40 * 1024 * 1024
CT = 8
GELU_C = math.sqrt(2.0 / math.pi)
GELU_A = 0.044715


def dot(a, b, ca, cb):
    return lax.dot_general(a, b, (((ca,), (cb,)), ((), ())), preferred_element_type=F32)


def write_edges(row, X, Y, ylo, yhi, corners):
    for x in range(X):
        ylo[0, x] = row(x, 0)
        yhi[0, x] = row(x, Y - 1)
    for i, x in enumerate((0, X - 1)):
        for j, y in enumerate((0, Y - 1)):
            corners[2 * i + j][0] = row(x, y)


def piece_shapes(S, X, Y, C, Z):
    return (
        [jax.ShapeDtypeStruct((S, Y, C, Z), BF16)] * X
        + [jax.ShapeDtypeStruct((S, X, C, Z), BF16)] * 2
        + [jax.ShapeDtypeStruct((S, C, Z), BF16)] * 4
    )


def piece_specs(X, Y, C, Z):
    return (
        [pl.BlockSpec((1, Y, C, Z), lambda s: (s, 0, 0, 0))] * X
        + [pl.BlockSpec((1, X, C, Z), lambda s: (s, 0, 0, 0))] * 2
        + [pl.BlockSpec((1, C, Z), lambda s: (s, 0, 0))] * 4
    )


def halo_specs(X, Y, C, Z):
    return (
        [pl.BlockSpec((1, Y, C, Z), lambda s: (s, 0, 0, 0))] * 2
        + [pl.BlockSpec((1, X, C, Z), lambda s: (s, 0, 0, 0))] * 2
        + [pl.BlockSpec((1, C, Z), lambda s: (s, 0, 0))] * 4
    )


def exchange_halo(pieces, X):
    planes, (ylo, yhi), corners = pieces[:X], pieces[X : X + 2], pieces[X + 2 :]
    nx, ny = lax.axis_size("gx"), lax.axis_size("gy")
    up_x = [(i, i + 1) for i in range(nx - 1)]
    up_y = [(i, i + 1) for i in range(ny - 1)]
    down_x = [(b, a) for a, b in up_x]
    down_y = [(b, a) for a, b in up_y]
    from_lo_x = lax.ppermute(planes[-1], "gx", up_x)
    from_hi_x = lax.ppermute(planes[0], "gx", down_x)
    from_lo_y = lax.ppermute(yhi, "gy", up_y)
    from_hi_y = lax.ppermute(ylo, "gy", down_y)
    got = []
    for i, dx in enumerate((-1, 1)):
        for j, dy in enumerate((-1, 1)):
            pairs = [
                ((x + dx) * ny + y + dy, x * ny + y)
                for x in range(nx)
                for y in range(ny)
                if 0 <= x + dx < nx and 0 <= y + dy < ny
            ]
            got.append(lax.ppermute(corners[2 * (1 - i) + (1 - j)], ("gx", "gy"), pairs))
    return [from_lo_x, from_hi_x, from_lo_y, from_hi_y] + got


def padded_rows(X, Y, planes, halo):
    xlo, xhi, ylo, yhi = halo[:4]
    corners = halo[4:]

    def row(x, y):
        ox, oy = (0 if x < 0 else 1 if x >= X else None), (0 if y < 0 else 1 if y >= Y else None)
        if ox is not None and oy is not None:
            return corners[2 * ox + oy][0]
        if ox is not None:
            return (xlo, xhi)[ox][0, y]
        if oy is not None:
            return (ylo, yhi)[oy][0, x]
        return planes[x][0, y]

    return row


def fill_taps(w_ref, wb, flip):
    C, Z = wb.shape[1:]
    for t in range(27):
        source = 26 - t if flip else t
        wb[t] = jnp.broadcast_to(w_ref[:, source : source + 1], (C, Z))


def fill_padded(row, Fs, X, Y):
    for x in range(-1, X + 1):
        for y in range(-1, Y + 1):
            Fs[(x + 1) * (Y + 2) + y + 1] = row(x, y).astype(F32)


def conv_tile(Fs, wb, channels, X, Y, lane, store):
    Z = Fs.shape[2]
    for x in range(X):
        for y in range(Y):
            acc = [None, None, None]
            for a in range(3):
                for b in range(3):
                    f = Fs[(x + a) * (Y + 2) + y + b, channels, :]
                    for e in range(3):
                        term = wb[(a * 3 + b) * 3 + e, channels, :] * f
                        acc[e] = term if acc[e] is None else acc[e] + term
            left = jnp.where(lane == 0, 0.0, pltpu.roll(acc[0], 1, 1))
            right = jnp.where(lane == Z - 1, 0.0, pltpu.roll(acc[2], Z - 1, 1))
            store(x, y, acc[1] + left + right)


def split_kernel(X, Y, C, Z, f_ref, *refs):
    planes, (ylo, yhi), corners = refs[:X], refs[X : X + 2], refs[X + 2 : X + 6]
    wide = refs[X + 6]
    wide[...] = f_ref[0].astype(F32)
    for x in range(X):
        for y in range(Y):
            planes[x][0, y] = wide[pl.ds(x * Y + y, C, stride=X * Y), :].astype(BF16)
    write_edges(lambda x, y: planes[x][0, y], X, Y, ylo, yhi, corners)


def main_kernel(dims, *refs):
    X, Y, C, Z, H, O = dims
    hx, NP = X // 2, Y // 4
    cells = X * Y * Z
    quarter = (Y // 2) * (Z // 2)
    planes, halo = refs[:X], refs[X : X + 8]
    gd_ref, w_ref, pinT_ref, pout_ref, wd_ref = refs[X + 8 : X + 13]
    outs = refs[X + 13 :]
    red_ref, gm_ref = outs[:2]
    d_planes, (d_ylo, d_yhi), d_corners = outs[2 : X + 2], outs[X + 2 : X + 4], outs[X + 4 : X + 8]
    packed_ref = outs[X + 8]
    Fs, wb, Ds, GMs, Mb, Pt, G1, adw, adown, aout, ain, pin, poutT = outs[X + 9 :]
    step = pl.program_id(0)

    @pl.when(step == 0)
    def _():
        fill_taps(w_ref, wb, False)
        adw[...] = jnp.zeros_like(adw)
        adown[...] = jnp.zeros_like(adown)
        aout[...] = jnp.zeros_like(aout)
        ain[...] = jnp.zeros_like(ain)
        pin[...] = pinT_ref[...].astype(F32).T.astype(BF16)
        poutT[...] = pout_ref[...].astype(F32).T.astype(BF16)

    fill_padded(padded_rows(X, Y, planes, halo), Fs, X, Y)
    lane = lax.broadcasted_iota(jnp.int32, (CT, Z), 1)

    fine = lax.broadcasted_iota(jnp.int32, (2 * Z, 2 * Z), 0)
    coarse = lax.broadcasted_iota(jnp.int32, (2 * Z, 2 * Z), 1)
    goes = (coarse // Z) * 1 + ((coarse % Z) % (Z // 2)) * 2 + ((coarse % Z) // (Z // 2)) * Z
    perm = jnp.where(fine == goes, 1.0, 0.0).astype(BF16)

    for X0 in range(hx):
        gp = dot(wd_ref[...], gd_ref[0, X0], 1, 1).astype(BF16)
        for a in range(2):
            for b in range(2):
                for p in range(NP):
                    src = ((a * 2 + b) * 2) * C
                    dst = ((a * 2 + b) * NP + p) * C
                    for e in range(2):
                        Mb[dst : dst + C, e * Z : (e + 1) * Z] = gp[
                            src + e * C : src + (e + 1) * C, p * Z : (p + 1) * Z
                        ]
        gm = dot(Mb[...], perm, 1, 1).astype(BF16)
        for a in range(2):
            for b in range(2):
                for p in range(NP):
                    src = ((a * 2 + b) * NP + p) * C
                    for q in range(2):
                        x, y = 2 * X0 + a, 2 * (2 * p + q) + b
                        value = gm[src : src + C, q * Z : (q + 1) * Z]
                        gm_ref[0, x, y] = value
                        r = x * Y + y
                        GMs[:, r * Z : (r + 1) * Z] = value

    def conv_body(i, carry):
        channels = pl.ds(pl.multiple_of(i * CT, CT), CT)

        def store(x, y, value):
            r = x * Y + y
            Ds[channels, r * Z : (r + 1) * Z] = value

        conv_tile(Fs, wb, channels, X, Y, lane, store)
        return carry

    lax.fori_loop(0, C // CT, conv_body, 0)

    width = 4 * Z

    for X0 in range(hx):

        def chunk_body(i, carry):
            a, p = i // NP, i % NP
            x = 2 * X0 + a
            columns = pl.ds(pl.multiple_of((x * NP + p) * width, width), width)
            depth = Ds[:, columns].astype(BF16)
            gm = GMs[:, columns]
            pre = dot(pin[...], depth, 1, 0)
            sq = pre * pre
            t = jnp.tanh(pre * (GELU_C + (GELU_C * GELU_A) * sq))
            h = 0.5 + 0.5 * t
            act = pre * h
            slope = h + act * (1.0 - h) * (2.0 * GELU_C + (6.0 * GELU_C * GELU_A) * sq)
            active = act.astype(BF16)
            branch = dot(pout_ref[...], active, 1, 0)
            for j in range(4):
                row = (x + 1) * (Y + 2) + 4 * p + j + 1
                merged = (Fs[row] + branch[:, j * Z : (j + 1) * Z]).astype(BF16)
                start = pl.multiple_of(((a * 2 + j % 2) * NP + p) * C, C)
                Mb[pl.ds(start, C), (j // 2) * Z : (j // 2 + 1) * Z] = merged
            grad_pre = (dot(poutT[...], gm, 1, 0) * slope).astype(BF16)
            grad_depth = dot(pinT_ref[...], grad_pre, 1, 0).astype(BF16).astype(F32)
            for j in range(4):
                G1[x * Y + 4 * p + j] = grad_depth[:, j * Z : (j + 1) * Z]
            aout[...] += dot(gm, active, 1, 1)
            ain[...] += dot(depth, grad_pre, 1, 1)
            return carry

        lax.fori_loop(0, 2 * NP, chunk_body, 0)

        pt = dot(Mb[...], perm, 1, 0).astype(BF16)
        for a in range(2):
            for b in range(2):
                for p in range(NP):
                    src = ((a * 2 + b) * NP + p) * C
                    for e in range(2):
                        dst = ((a * 2 + b) * 2 + e) * C
                        Pt[dst : dst + C, p * Z : (p + 1) * Z] = pt[
                            src : src + C, e * Z : (e + 1) * Z
                        ]
        red_ref[0, X0] = dot(Pt[...], wd_ref[...], 0, 0).astype(BF16)
        adown[...] += dot(Pt[...], gd_ref[0, X0], 1, 0)

    def grad_row(x, y):
        return G1[x * Y + y].astype(BF16)

    for x in range(X):
        for y in range(Y):
            d_planes[x][0, y] = grad_row(x, y)
    write_edges(grad_row, X, Y, d_ylo, d_yhi, d_corners)

    def tap_body(i, carry):
        channels = pl.ds(pl.multiple_of(i * CT, CT), CT)
        sums = [None] * 27
        for x in range(X):
            for y in range(Y):
                g = G1[x * Y + y, channels, :]
                gs = (
                    jnp.where(lane == Z - 1, 0.0, pltpu.roll(g, Z - 1, 1)),
                    g,
                    jnp.where(lane == 0, 0.0, pltpu.roll(g, 1, 1)),
                )
                for a in range(3):
                    for b in range(3):
                        f = Fs[(x + a) * (Y + 2) + y + b, channels, :]
                        for e in range(3):
                            t = (a * 3 + b) * 3 + e
                            term = gs[e] * f
                            sums[t] = term if sums[t] is None else sums[t] + term
        for t in range(27):
            adw[t, channels, :] += sums[t]
        return carry

    lax.fori_loop(0, C // CT, tap_body, 0)

    @pl.when(step == pl.num_programs(0) - 1)
    def _():
        columns = lax.broadcasted_iota(jnp.int32, (C, Z), 1)
        taps = jnp.zeros((C, Z), F32)
        for t in range(27):
            taps = jnp.where(columns == t, jnp.sum(adw[t], axis=1, keepdims=True), taps)
        at = 0
        for block in (
            [adown[...]]
            + [aout[:, k : k + Z] for k in range(0, H, Z)]
            + [ain[:, k : k + Z] for k in range(0, H, Z)]
            + [taps]
        ):
            packed_ref[at : at + block.shape[0], :] = block.astype(BF16)
            at += block.shape[0]
        if at < packed_ref.shape[0]:
            rest = packed_ref.shape[0] - at
            packed_ref[at:, :] = jnp.zeros((rest, Z), BF16)


def adjoint_kernel(X, Y, C, Z, *refs):
    planes, halo = refs[:X], refs[X : X + 8]
    gm_ref, w_ref, out_ref, Fs, wb, wide = refs[X + 8 :]

    @pl.when(pl.program_id(0) == 0)
    def _():
        fill_taps(w_ref, wb, True)

    fill_padded(padded_rows(X, Y, planes, halo), Fs, X, Y)
    lane = lax.broadcasted_iota(jnp.int32, (CT, Z), 1)
    rows = X * Y

    def conv_body(i, carry):
        first = pl.multiple_of(i * CT, CT)
        channels = pl.ds(first, CT)

        def store(x, y, value):
            r = x * Y + y
            total = value + gm_ref[0, x, y, channels, :].astype(F32)
            wide[pl.ds(first * rows + r, CT, stride=rows), :] = total

        conv_tile(Fs, wb, channels, X, Y, lane, store)
        return carry

    lax.fori_loop(0, C // CT, conv_body, 0)
    out_ref[0] = wide[...].astype(BF16)


def swap_in_group(blocks, axis):
    g = blocks.shape[0]
    if g == 1:
        return blocks
    n = lax.axis_size(axis)
    member = lax.axis_index(axis) % g
    got = [lax.dynamic_index_in_dim(blocks, member, 0, keepdims=False)]
    for k in range(1, g):
        out = lax.dynamic_index_in_dim(blocks, (member + k) % g, 0, keepdims=False)
        pairs = [(i, i - i % g + (i + k) % g) for i in range(n)]
        got.append(lax.ppermute(out, axis, pairs))
    if g == 2:
        first = member == 0
        return jnp.stack([jnp.where(first, got[0], got[1]), jnp.where(first, got[1], got[0])])
    got = jnp.stack(got)
    return jnp.take(got, (member - jnp.arange(g, dtype=jnp.int32)) % g, axis=0)


def sum_over_devices(packed, devices):
    axes = ("gx", "gy")
    lanes = packed.shape[1]
    mine = lax.all_to_all(packed.reshape(devices, -1, lanes), axes, 0, 0)
    total = jnp.sum(mine.astype(F32), axis=0).astype(BF16)
    every = lax.all_to_all(jnp.broadcast_to(total[None], (devices,) + total.shape), axes, 0, 0)
    return every.reshape(-1, lanes).astype(F32)


def per_device(fields, depth_kernel, point_in, point_out, down_kernel, cotangent):
    S, C, X, Y, Z = fields.shape
    H, O = point_in.shape[0], down_kernel.shape[0]
    hx, hy, hz = X // 2, Y // 2, Z // 2
    nx, ny = lax.axis_size("gx"), lax.axis_size("gy")
    devices = nx * ny
    gx, gy = nx // GRIDC, ny // GRIDC
    per_group = S // (gx * gy)
    params = pltpu.CompilerParams(
        dimension_semantics=("arbitrary",), vmem_limit_bytes=VMEM_LIMIT
    )

    pieces = pl.pallas_call(
        functools.partial(split_kernel, X, Y, C, Z),
        grid=(S,),
        in_specs=[pl.BlockSpec((1, C * X * Y, Z), lambda s: (s, 0, 0))],
        out_specs=piece_specs(X, Y, C, Z),
        out_shape=piece_shapes(S, X, Y, C, Z),
        scratch_shapes=[pltpu.VMEM((C * X * Y, Z), F32)],
        compiler_params=params,
        name="split_fields",
    )(fields.reshape(S, C * X * Y, Z))

    halo = exchange_halo(pieces, X)

    moved = cotangent[0, 0].transpose(0, 2, 3, 4, 1)
    moved = moved.reshape(per_group, gx * hx, gy, hy * hz, O).transpose(2, 0, 1, 3, 4)
    moved = swap_in_group(moved, "gy").reshape(gy * per_group, gx, hx, hy * hz, O)
    moved = swap_in_group(moved.transpose(1, 0, 2, 3, 4), "gx")
    grad_down = moved.reshape(S, hx, hy * hz, O)

    wd = down_kernel.transpose(2, 3, 4, 1, 0).reshape(8 * C, O)
    taps = depth_kernel.reshape(C, 27).astype(F32)

    rows = 8 * C + 2 * C * (H // Z) + C
    chunk = -(-rows // (16 * devices)) * 16
    cells = X * Y * Z
    whole = lambda shape: pl.BlockSpec(shape, lambda s: (0,) * len(shape))
    flops = S * cells * (2 * 6 * C * H + 2 * 3 * C * O + 2 * 2 * 27 * C)
    out = pl.pallas_call(
        functools.partial(main_kernel, (X, Y, C, Z, H, O)),
        grid=(S,),
        in_specs=[pl.BlockSpec((1, Y, C, Z), lambda s: (s, 0, 0, 0))] * X
        + halo_specs(X, Y, C, Z)
        + [
            pl.BlockSpec((1, hx, hy * hz, O), lambda s: (s, 0, 0, 0)),
            whole((C, 27)),
            whole((C, H)),
            whole((C, H)),
            whole((8 * C, O)),
        ],
        out_specs=[
            pl.BlockSpec((1, hx, hy * hz, O), lambda s: (s, 0, 0, 0)),
            pl.BlockSpec((1, X, Y, C, Z), lambda s: (s, 0, 0, 0, 0)),
        ]
        + piece_specs(X, Y, C, Z)
        + [whole((devices * chunk, Z))],
        out_shape=[
            jax.ShapeDtypeStruct((S, hx, hy * hz, O), BF16),
            jax.ShapeDtypeStruct((S, X, Y, C, Z), BF16),
        ]
        + piece_shapes(S, X, Y, C, Z)
        + [jax.ShapeDtypeStruct((devices * chunk, Z), BF16)],
        scratch_shapes=[
            pltpu.VMEM(((X + 2) * (Y + 2), C, Z), F32),
            pltpu.VMEM((27, C, Z), F32),
            pltpu.VMEM((C, cells), F32),
            pltpu.VMEM((C, cells), BF16),
            pltpu.VMEM((Y * C, 2 * Z), BF16),
            pltpu.VMEM((8 * C, hy * hz), BF16),
            pltpu.VMEM((X * Y, C, Z), F32),
            pltpu.VMEM((27, C, Z), F32),
            pltpu.VMEM((8 * C, O), F32),
            pltpu.VMEM((C, H), F32),
            pltpu.VMEM((C, H), F32),
            pltpu.VMEM((H, C), BF16),
            pltpu.VMEM((H, C), BF16),
        ],
        compiler_params=params,
        cost_estimate=pl.CostEstimate(
            flops=flops, bytes_accessed=8 * S * cells * C, transcendentals=S * cells * H
        ),
        name="main",
    )(*pieces[:X], *halo, grad_down, taps, point_in.T, point_out, wd)
    reduced, grad_merged = out[:2]
    grad_pieces = out[2 : X + 8]
    packed = out[X + 8]

    grad_halo = exchange_halo(grad_pieces, X)

    total = sum_over_devices(packed, devices)

    grad_fields = pl.pallas_call(
        functools.partial(adjoint_kernel, X, Y, C, Z),
        grid=(S,),
        in_specs=[pl.BlockSpec((1, Y, C, Z), lambda s: (s, 0, 0, 0))] * X
        + halo_specs(X, Y, C, Z)
        + [pl.BlockSpec((1, X, Y, C, Z), lambda s: (s, 0, 0, 0, 0)), whole((C, 27))],
        out_specs=pl.BlockSpec((1, C * X * Y, Z), lambda s: (s, 0, 0)),
        out_shape=jax.ShapeDtypeStruct((S, C * X * Y, Z), BF16),
        scratch_shapes=[
            pltpu.VMEM(((X + 2) * (Y + 2), C, Z), F32),
            pltpu.VMEM((27, C, Z), F32),
            pltpu.VMEM((C * X * Y, Z), F32),
        ],
        compiler_params=params,
        cost_estimate=pl.CostEstimate(
            flops=S * cells * 2 * 27 * C, bytes_accessed=8 * S * cells * C, transcendentals=0
        ),
        name="adjoint",
    )(*grad_pieces[:X], *grad_halo, grad_merged, taps).reshape(S, C, X, Y, Z)

    moved = swap_in_group(reduced.reshape(gx, S // gx, hx, hy * hz, O), "gx")
    moved = moved.transpose(1, 0, 2, 3, 4).reshape(gy, per_group, gx * hx, hy * hz, O)
    moved = swap_in_group(moved, "gy").transpose(1, 2, 0, 3, 4)
    coarse = moved.reshape(per_group, gx * hx, gy * hy, hz, O).transpose(0, 4, 1, 2, 3)[None, None]

    total = total * (1.0 / math.sqrt(S * cells * devices))
    at = 8 * C
    grad_down_kernel = total[:at].reshape(2, 2, 2, C, O).transpose(4, 3, 0, 1, 2)
    wide = C * (H // Z)
    halves = total[at : at + 2 * wide].reshape(2, H // Z, C, Z).transpose(0, 2, 1, 3)
    halves = halves.reshape(2, C, H)
    grad_depth_kernel = total[at + 2 * wide : rows, :27].reshape(C, 3, 3, 3)
    return (
        coarse,
        grad_fields,
        grad_depth_kernel,
        halves[1].T,
        halves[0],
        grad_down_kernel,
    )


def solution(mesh):
    placed = (
        P(None, None, "gx", "gy", None),
        P(),
        P(),
        P(),
        P(),
        P("gx", "gy", None, None, None, None, None),
    )
    return jax.shard_map(
        per_device,
        mesh=mesh,
        in_specs=placed,
        out_specs=(
            P("gx", "gy", None, None, None, None, None),
            P(None, None, "gx", "gy", None),
            P(),
            P(),
            P(),
            P(),
        ),
        check_vma=False,
    )
```

time: 367 us -> 102 us (0.28)
  the two profiles are of different devices: /device:TPU:0 before, /device:TPU:4 now
where the time goes in v1:
time: 102 us; the launch traced here: 101 us
  starting transfers between devices  51.8 us (51%)
  Pallas kernels  19.5 us (19%)
  blocking collectives  13.5 us (13%)
  waiting for transfers between devices  9.03 us (9%)
  local copies, waits for them, and re-layouts  5.21 us (5%)
  between operations  1.06 us (1%)
    ppermute x8, starting transfers between devices, exchange_halo(): lax.ppermute(corners[2 * (1 - i) + (1 - j)], ('gx', 'gy'), pairs)  24.2 us
    pallas_call x1, Pallas kernels, per_device(): pl.pallas_call(functools.partial(main_kernel, (X, Y, C, Z, H, O)), grid=(...  15.3 us
    all_to_all x1, blocking collectives, sum_over_devices(): mine = lax.all_to_all(packed.reshape(devices, -1, lanes), axes, 0, 0)  13.5 us
    ppermute x2, starting transfers between devices, exchange_halo(): from_lo_y = lax.ppermute(yhi, 'gy', up_y)  12.7 us
    ppermute x2, waiting for transfers between devices, exchange_halo(): from_hi_y = lax.ppermute(ylo, 'gy', down_y)  8.47 us
    ppermute x2, starting transfers between devices, exchange_halo(): from_lo_x = lax.ppermute(planes[-1], 'gx', up_x)  4.35 us
    ppermute x2, starting transfers between devices, exchange_halo(): from_hi_x = lax.ppermute(planes[0], 'gx', down_x)  4.31 us
    pallas_call x1, Pallas kernels, per_device(): pl.pallas_call(functools.partial(adjoint_kernel, X, Y, C, Z), grid=(S,),...  3.85 us
  transfers between devices with their start and end apart: 19, of which 3 were waited for; matrix products, arithmetic and copies ran while one was open for 1% of the time, Pallas kernels for 4%

profile of v1, /device:TPU:4, one launch (start us, length us, event | category | flops | bytes accessed | tf_op | source)
XLA Modules:
  0.0 101.0 jit_solution(12658304652710136255)
XLA Ops:
  0.7 0.8 dynamic-slice_bitcast_fusion
  1.5 0.0 collective-permute-start.8
  1.5 0.0 copy-start
  1.5 1.0 %copy-done = bf16[2,64,2,8,128]{4,3,2,1,0:T(8,128)(2,1)S(1)} copy-done((bf16[2,64,2,8,128]{4,3,2,1,0:T(8,128)(2,1)S(1)}, bf16[2,64,2,8,128]{4,3,2,1,0:T(8,128)(2,1)}, u32[]{:S(2)}) %copy-start) | copy-done | bytes 524312
  2.6 0.4 split_fields.1
  3.0 0.0 copy-start.5
  3.0 3.6 %collective-permute-start.4 = (bf16[2,64,128]{2,1,0:T(8,128)(2,1)S(1)}, bf16[2,64,128]{2,1,0:T(8,128)(2,1)S(1)}, u32[]{:S(2)}, u32[]{:S(2)}) collective-permute-start(bf16[2,64,128]{2,1,0:T(8,128)(2,1)S(1)} %get-tuple-element.29), channel_id=1, source_target_pairs={{0,5},{1,6},{2,7},{4,9},{5,10},{6,11},{8,13},{9,14},{10,15},{12,17... | collective-permute-start | bytes 98312 | tf_op jit(solution)/shard_map/ppermute | solution.py:77
  6.6 1.3 %collective-permute-start.5 = (bf16[2,64,128]{2,1,0:T(8,128)(2,1)S(1)}, bf16[2,64,128]{2,1,0:T(8,128)(2,1)S(1)}, u32[]{:S(2)}, u32[]{:S(2)}) collective-permute-start(bf16[2,64,128]{2,1,0:T(8,128)(2,1)S(1)} %get-tuple-element.30), channel_id=1, source_target_pairs={{1,4},{2,5},{3,6},{5,8},{6,9},{7,10},{9,12},{10,13},{11,14},{13,16... | collective-permute-start | bytes 98312 | tf_op jit(solution)/shard_map/ppermute | solution.py:77
  7.9 6.1 %collective-permute-start.6 = (bf16[2,64,128]{2,1,0:T(8,128)(2,1)S(1)}, bf16[2,64,128]{2,1,0:T(8,128)(2,1)S(1)}, u32[]{:S(2)}, u32[]{:S(2)}) collective-permute-start(bf16[2,64,128]{2,1,0:T(8,128)(2,1)S(1)} %get-tuple-element.31), channel_id=1, source_target_pairs={{4,1},{5,2},{6,3},{8,5},{9,6},{10,7},{12,9},{13,10},{14,11},{16,13... | collective-permute-start | bytes 98312 | tf_op jit(solution)/shard_map/ppermute | solution.py:77
  14.0 2.1 %collective-permute-start.1 = (bf16[2,8,64,128]{3,2,1,0:T(8,128)(2,1)S(1)}, bf16[2,8,64,128]{3,2,1,0:T(8,128)(2,1)S(1)}, u32[]{:S(2)}, u32[]{:S(2)}) collective-permute-start(bf16[2,8,64,128]{3,2,1,0:T(8,128)(2,1)S(1)} %get-tuple-element.25.refs_0_), channel_id=1, source_target_pairs={{4,0},{8,4},{12,8},{16,12},{20,16},{24,20},{28,24},{5,1},{9,5},{13... | collective-permute-start | bytes 786440 | tf_op jit(solution)/shard_map/ppermute | solution.py:65
  16.1 0.0 copy-done.5
  16.1 0.1 copy.29.refs_11_
  16.2 0.0 copy-done.3
  16.2 0.0 collective-permute-done.8
  16.2 2.2 %collective-permute-start = (bf16[2,8,64,128]{3,2,1,0:T(8,128)(2,1)S(1)}, bf16[2,8,64,128]{3,2,1,0:T(8,128)(2,1)S(1)}, u32[]{:S(2)}, u32[]{:S(2)}) collective-permute-start(bf16[2,8,64,128]{3,2,1,0:T(8,128)(2,1)S(1)} %get-tuple-element.26.refs_1_), channel_id=1, source_target_pairs={{0,4},{4,8},{8,12},{12,16},{16,20},{20,24},{24,28},{1,5},{5,9},{9,... | collective-permute-start | bytes 786440 | tf_op jit(solution)/shard_map/ppermute | solution.py:64
  18.5 0.0 copy-done.4
  18.5 0.0 collective-permute-done.4.refs_6_
  18.5 1.3 %collective-permute-start.7 = (bf16[2,64,128]{2,1,0:T(8,128)(2,1)S(1)}, bf16[2,64,128]{2,1,0:T(8,128)(2,1)S(1)}, u32[]{:S(2)}, u32[]{:S(2)}) collective-permute-start(bf16[2,64,128]{2,1,0:T(8,128)(2,1)S(1)} %get-tuple-element.32), channel_id=1, source_target_pairs={{5,0},{6,1},{7,2},{9,4},{10,5},{11,6},{13,8},{14,9},{15,10},{17,12... | collective-permute-start | bytes 98312 | tf_op jit(solution)/shard_map/ppermute | solution.py:77
  19.8 0.0 collective-permute-done.5.refs_7_
  19.8 6.3 %collective-permute-start.2 = (bf16[2,2,64,128]{3,2,1,0:T(8,128)(2,1)S(1)}, bf16[2,2,64,128]{3,2,1,0:T(8,128)(2,1)S(1)}, u32[]{:S(2)}, u32[]{:S(2)}) collective-permute-start(bf16[2,2,64,128]{3,2,1,0:T(8,128)(2,1)S(1)} %get-tuple-element.27), channel_id=1, source_target_pairs={{0,1},{1,2},{2,3},{4,5},{5,6},{6,7},{8,9},{9,10},{10,11},{12,13},{... | collective-permute-start | bytes 196616 | tf_op jit(solution)/shard_map/ppermute | solution.py:66
  26.1 0.0 collective-permute-done.6.refs_8_
  26.2 1.3 %collective-permute-start.3 = (bf16[2,2,64,128]{3,2,1,0:T(8,128)(2,1)S(1)}, bf16[2,2,64,128]{3,2,1,0:T(8,128)(2,1)S(1)}, u32[]{:S(2)}, u32[]{:S(2)}) collective-permute-start(bf16[2,2,64,128]{3,2,1,0:T(8,128)(2,1)S(1)} %get-tuple-element.28), channel_id=1, source_target_pairs={{1,0},{2,1},{3,2},{5,4},{6,5},{7,6},{9,8},{10,9},{11,10},{13,12},{... | collective-permute-start | bytes 196616 | tf_op jit(solution)/shard_map/ppermute | solution.py:67
  27.5 0.0 copy-start.1
  27.5 0.0 copy-start.2
  27.5 0.0 collective-permute-done.7.refs_9_
  27.5 0.5 collective-permute-done.2.refs_4_
  28.0 4.3 %collective-permute-done.3.refs_5_ = bf16[2,2,64,128]{3,2,1,0:T(8,128)(2,1)S(1)} collective-permute-done((bf16[2,2,64,128]{3,2,1,0:T(8,128)(2,1)S(1)}, bf16[2,2,64,128]{3,2,1,0:T(8,128)(2,1)S(1)}, u32[]{:S(2)}, u32[]{:S(2)}) %collective-permute-start.3) | collective-permute-done | bytes 65568 | tf_op jit(solution)/shard_map/ppermute | solution.py:67
  32.3 0.0 collective-permute-done.1.refs_3_
  32.3 0.0 collective-permute-done.refs_2_
  32.3 0.0 copy-done.1
  32.3 0.0 copy-done.2
  32.3 15.3 %main.1 = (bf16[2,1,256,128]{3,2,1,0:T(8,128)(2,1)S(1)}, bf16[2,2,8,64,128]{4,3,2,1,0:T(8,128)(2,1)S(1)}, bf16[2,8,64,128]{3,2,1,0:T(8,128)(2,1)S(1)}, bf16[2,8,...) custom-call(bf16[2,8,64,128]{3,2,1,0:T(8,128)(2,1)S(1)} %get-tuple-e, ...), custom_call_target="tpu_custom_call" | custom-call | flops 1034944512 | bytes 2097152 | tf_op jit(solution)/shard_map/main/pallas_call | solution.py:396
  47.6 13.5 %all_to_all.10 = bf16[32,32,128]{2,1,0:T(8,128)(2,1)S(1)} all-to-all(bf16[32,32,128]{2,1,0:T(8,128)(2,1)S(1)} %bitcast.58), channel_id=1, replica_groups=mesh['gx'=8,'gy'=4] {'gx','gy'}, dimensions={0} | all-to-all | bytes 524288 | tf_op jit(solution)/shard_map/all_to_all | solution.py:351
  61.1 0.1 reduce_sum.12
  61.1 0.7 broadcast_in_dim.10
  61.9 3.4 %all-to-all-start.1 = ((bf16[32,32,128]{2,1,0:T(8,128)(2,1)}), bf16[32,32,128]{2,1,0:T(8,128)(2,1)S(1)}, u32[]{:S(2)}, u32[]{:S(2)}) async-start(bf16[32,32,128]{2,1,0:T(8,128)(2,1)} %broadcast_in_dim.10), calls=%async_computation.1 | async-start | bytes 524288 | tf_op jit(solution)/shard_map/all_to_all | solution.py:353
  65.3 0.2 collective-permute-start.9
  65.6 3.3 %collective-permute-start.14 = (bf16[2,64,128]{2,1,0:T(8,128)(2,1)S(1)}, bf16[2,64,128]{2,1,0:T(8,128)(2,1)S(1)}, u32[]{:S(2)}, u32[]{:S(2)}) collective-permute-start(bf16[2,64,128]{2,1,0:T(8,128)(2,1)S(1)} %get-tuple-element.38), channel_id=1, source_target_pairs={{0,5},{1,6},{2,7},{4,9},{5,10},{6,11},{8,13},{9,14},{10,15},{12,17... | collective-permute-start | bytes 98312 | tf_op jit(solution)/shard_map/ppermute | solution.py:77
  68.9 1.3 %collective-permute-start.15 = (bf16[2,64,128]{2,1,0:T(8,128)(2,1)S(1)}, bf16[2,64,128]{2,1,0:T(8,128)(2,1)S(1)}, u32[]{:S(2)}, u32[]{:S(2)}) collective-permute-start(bf16[2,64,128]{2,1,0:T(8,128)(2,1)S(1)} %get-tuple-element.39), channel_id=1, source_target_pairs={{1,4},{2,5},{3,6},{5,8},{6,9},{7,10},{9,12},{10,13},{11,14},{13,16... | collective-permute-start | bytes 98312 | tf_op jit(solution)/shard_map/ppermute | solution.py:77
  70.2 6.1 %collective-permute-start.16 = (bf16[2,64,128]{2,1,0:T(8,128)(2,1)S(1)}, bf16[2,64,128]{2,1,0:T(8,128)(2,1)S(1)}, u32[]{:S(2)}, u32[]{:S(2)}) collective-permute-start(bf16[2,64,128]{2,1,0:T(8,128)(2,1)S(1)} %get-tuple-element.40), channel_id=1, source_target_pairs={{4,1},{5,2},{6,3},{8,5},{9,6},{10,7},{12,9},{13,10},{14,11},{16,13... | collective-permute-start | bytes 98312 | tf_op jit(solution)/shard_map/ppermute | solution.py:77
  76.3 2.2 %collective-permute-start.11 = (bf16[2,8,64,128]{3,2,1,0:T(8,128)(2,1)S(1)}, bf16[2,8,64,128]{3,2,1,0:T(8,128)(2,1)S(1)}, u32[]{:S(2)}, u32[]{:S(2)}) collective-permute-start(bf16[2,8,64,128]{3,2,1,0:T(8,128)(2,1)S(1)} %get-tuple-element.34.refs_0_), channel_id=1, source_target_pairs={{4,0},{8,4},{12,8},{16,12},{20,16},{24,20},{28,24},{5,1},{9,5},{13... | collective-permute-start | bytes 786440 | tf_op jit(solution)/shard_map/ppermute | solution.py:65
  78.5 0.0 collective-permute-done.9
  78.5 2.1 %collective-permute-start.10 = (bf16[2,8,64,128]{3,2,1,0:T(8,128)(2,1)S(1)}, bf16[2,8,64,128]{3,2,1,0:T(8,128)(2,1)S(1)}, u32[]{:S(2)}, u32[]{:S(2)}) collective-permute-start(bf16[2,8,64,128]{3,2,1,0:T(8,128)(2,1)S(1)} %get-tuple-element.35.refs_1_), channel_id=1, source_target_pairs={{0,4},{4,8},{8,12},{12,16},{16,20},{20,24},{24,28},{1,5},{5,9},{9,... | collective-permute-start | bytes 786440 | tf_op jit(solution)/shard_map/ppermute | solution.py:64
  80.6 0.0 collective-permute-done.14.refs_6_
  80.7 1.3 %collective-permute-start.17 = (bf16[2,64,128]{2,1,0:T(8,128)(2,1)S(1)}, bf16[2,64,128]{2,1,0:T(8,128)(2,1)S(1)}, u32[]{:S(2)}, u32[]{:S(2)}) collective-permute-start(bf16[2,64,128]{2,1,0:T(8,128)(2,1)S(1)} %get-tuple-element.41), channel_id=1, source_target_pairs={{5,0},{6,1},{7,2},{9,4},{10,5},{11,6},{13,8},{14,9},{15,10},{17,12... | collective-permute-start | bytes 98312 | tf_op jit(solution)/shard_map/ppermute | solution.py:77
  82.0 0.0 collective-permute-done.15.refs_7_
  82.0 6.4 %collective-permute-start.12 = (bf16[2,2,64,128]{3,2,1,0:T(8,128)(2,1)S(1)}, bf16[2,2,64,128]{3,2,1,0:T(8,128)(2,1)S(1)}, u32[]{:S(2)}, u32[]{:S(2)}) collective-permute-start(bf16[2,2,64,128]{3,2,1,0:T(8,128)(2,1)S(1)} %get-tuple-element.36), channel_id=1, source_target_pairs={{0,1},{1,2},{2,3},{4,5},{5,6},{6,7},{8,9},{9,10},{10,11},{12,13},{... | collective-permute-start | bytes 196616 | tf_op jit(solution)/shard_map/ppermute | solution.py:66
  88.4 0.0 collective-permute-done.16.refs_8_
  88.4 1.3 %collective-permute-start.13 = (bf16[2,2,64,128]{3,2,1,0:T(8,128)(2,1)S(1)}, bf16[2,2,64,128]{3,2,1,0:T(8,128)(2,1)S(1)}, u32[]{:S(2)}, u32[]{:S(2)}) collective-permute-start(bf16[2,2,64,128]{3,2,1,0:T(8,128)(2,1)S(1)} %get-tuple-element.37), channel_id=1, source_target_pairs={{1,0},{2,1},{3,2},{5,4},{6,5},{7,6},{9,8},{10,9},{11,10},{13,12},{... | collective-permute-start | bytes 196616 | tf_op jit(solution)/shard_map/ppermute | solution.py:67
  89.7 0.7 maximum_bitcast_fusion.1
  90.4 0.0 collective-permute-done.17.refs_9_
  90.4 0.0 collective-permute-done.12.refs_4_
  90.4 4.2 %collective-permute-done.13.refs_5_ = bf16[2,2,64,128]{3,2,1,0:T(8,128)(2,1)S(1)} collective-permute-done((bf16[2,2,64,128]{3,2,1,0:T(8,128)(2,1)S(1)}, bf16[2,2,64,128]{3,2,1,0:T(8,128)(2,1)S(1)}, u32[]{:S(2)}, u32[]{:S(2)}) %collective-permute-start.13) | collective-permute-done | bytes 65568 | tf_op jit(solution)/shard_map/ppermute | solution.py:67
  94.6 0.0 collective-permute-done.11.refs_3_
  94.6 0.0 collective-permute-done.10.refs_2_
  94.6 3.9 %adjoint.1 = bf16[2,1024,128]{2,1,0:T(8,128)(2,1)} custom-call(bf16[2,8,64,128]{3,2,1,0:T(8,128)(2,1)S(1)} %get-tuple-element.34.refs_0_, bf16[2,8,64,128]{3,2,1,0:T(8,128)(2,1)S(1)} %get-tuple-element.35.refs_1_, bf16[2,8,64,128]{3,2,1,0:T(8,128)(2,1)S(1)} %collective-permute-done.10.refs_2_, bf16[2,8,64,128]{3,2,1,0:T(8,128)(2,1)S(1)} %collective-permute-done.11.refs_3_, ...), custom_call_target="tpu_custom_call" | custom-call | flops 14155776 | bytes 2097152 | tf_op jit(solution)/shard_map/adjoint/pallas_call | solution.py:449
  98.4 0.0 all-to-all-done.1
  98.4 0.1 convert_multiply_fusion
  98.6 0.1 copy.31
  98.6 0.6 reshape.67
  99.3 0.9 copy.34
  100.2 0.1 copy.33
  100.2 0.1 copy.32
  100.3 0.7 copy_bitcast_fusion
  (12 shorter events, 0.1 us)
Async XLA Ops:
  1.5 14.7 %collective-permute-start.8 = (bf16[1,1,256,128]{3,2,1,0:T(8,128)(2,1)S(1)}, bf16[1,1,256,128]{3,2,1,0:T(8,128)(2,1)S(1)}, u32[]{:S(2)}, u32[]{:S(2)}) collective-permute-start(bf16[1,1,256,128]{3,2,1,0:T(8,128)(2,1)S(1)} %dynamic-slice_bitcast_fusion), channel_id=1, source_target_pairs={{0,4},{4,0},{8,12},{12,8},{16,20},{20,16},{24,28},{28,24},{1,5},{5... | collective-permute-start | bytes 196616 | tf_op jit(solution)/shard_map/ppermute | solution.py:340
  1.5 1.0 %copy-start = (bf16[2,64,2,8,128]{4,3,2,1,0:T(8,128)(2,1)S(1)}, bf16[2,64,2,8,128]{4,3,2,1,0:T(8,128)(2,1)}, u32[]{:S(2)}) copy-start(bf16[2,64,2,8,128]{4,3,2,1,0:T(8,128)(2,1)} %param.6) | copy-start | bytes 1572868
  2.5 13.6 %copy-start.3 = (bf16[128,64,2,2,2]{0,4,3,2,1:T(2,128)(2,1)S(1)}, bf16[128,64,2,2,2]{0,4,3,2,1:T(2,128)(2,1)}, u32[]{:S(2)}) copy-start(bf16[128,64,2,2,2]{0,4,3,2,1:T(2,128)(2,1)} %param.10) | copy-start | bytes 393220
  3.0 13.1 %copy-start.5 = (bf16[64,3,3,3]{0,3,2,1:T(4,128)(2,1)S(1)}, bf16[64,3,3,3]{0,3,2,1:T(4,128)(2,1)}, u32[]{:S(2)}) copy-start(bf16[64,3,3,3]{0,3,2,1:T(4,128)(2,1)} %param.7) | copy-start | bytes 10372
  3.0 15.5 %collective-permute-start.4 = (bf16[2,64,128]{2,1,0:T(8,128)(2,1)S(1)}, bf16[2,64,128]{2,1,0:T(8,128)(2,1)S(1)}, u32[]{:S(2)}, u32[]{:S(2)}) collective-permute-start(bf16[2,64,128]{2,1,0:T(8,128)(2,1)S(1)} %get-tuple-element.29), channel_id=1, source_target_pairs={{0,5},{1,6},{2,7},{4,9},{5,10},{6,11},{8,13},{9,14},{10,15},{12,17... | collective-permute-start | bytes 98312 | tf_op jit(solution)/shard_map/ppermute | solution.py:77
  6.6 13.2 %collective-permute-start.5 = (bf16[2,64,128]{2,1,0:T(8,128)(2,1)S(1)}, bf16[2,64,128]{2,1,0:T(8,128)(2,1)S(1)}, u32[]{:S(2)}, u32[]{:S(2)}) collective-permute-start(bf16[2,64,128]{2,1,0:T(8,128)(2,1)S(1)} %get-tuple-element.30), channel_id=1, source_target_pairs={{1,4},{2,5},{3,6},{5,8},{6,9},{7,10},{9,12},{10,13},{11,14},{13,16... | collective-permute-start | bytes 98312 | tf_op jit(solution)/shard_map/ppermute | solution.py:77
  7.9 18.3 %collective-permute-start.6 = (bf16[2,64,128]{2,1,0:T(8,128)(2,1)S(1)}, bf16[2,64,128]{2,1,0:T(8,128)(2,1)S(1)}, u32[]{:S(2)}, u32[]{:S(2)}) collective-permute-start(bf16[2,64,128]{2,1,0:T(8,128)(2,1)S(1)} %get-tuple-element.31), channel_id=1, source_target_pairs={{4,1},{5,2},{6,3},{8,5},{9,6},{10,7},{12,9},{13,10},{14,11},{16,13... | collective-permute-start | bytes 98312 | tf_op jit(solution)/shard_map/ppermute | solution.py:77
  14.0 18.4 %collective-permute-start.1 = (bf16[2,8,64,128]{3,2,1,0:T(8,128)(2,1)S(1)}, bf16[2,8,64,128]{3,2,1,0:T(8,128)(2,1)S(1)}, u32[]{:S(2)}, u32[]{:S(2)}) collective-permute-start(bf16[2,8,64,128]{3,2,1,0:T(8,128)(2,1)S(1)} %get-tuple-element.25.refs_0_), channel_id=1, source_target_pairs={{4,0},{8,4},{12,8},{16,12},{20,16},{24,20},{28,24},{5,1},{9,5},{13... | collective-permute-start | bytes 786440 | tf_op jit(solution)/shard_map/ppermute | solution.py:65
  16.2 2.3 %copy-start.4 = (bf16[1,1,1,128,2,4,64]{3,6,5,4,2,1,0:T(8,128)(2,1)S(1)}, bf16[1,1,1,128,2,4,64]{3,6,5,4,2,1,0:T(8,128)(2,1)}, u32[]{:S(2)}) copy-start(bf16[1,1,1,128,2,4,64]{3,6,5,4,2,1,0:T(8,128)(2,1)} %param.11) | copy-start | bytes 393220
  16.2 16.1 %collective-permute-start = (bf16[2,8,64,128]{3,2,1,0:T(8,128)(2,1)S(1)}, bf16[2,8,64,128]{3,2,1,0:T(8,128)(2,1)S(1)}, u32[]{:S(2)}, u32[]{:S(2)}) collective-permute-start(bf16[2,8,64,128]{3,2,1,0:T(8,128)(2,1)S(1)} %get-tuple-element.26.refs_1_), channel_id=1, source_target_pairs={{0,4},{4,8},{8,12},{12,16},{16,20},{20,24},{24,28},{1,5},{5,9},{9,... | collective-permute-start | bytes 786440 | tf_op jit(solution)/shard_map/ppermute | solution.py:64
  18.5 9.0 %collective-permute-start.7 = (bf16[2,64,128]{2,1,0:T(8,128)(2,1)S(1)}, bf16[2,64,128]{2,1,0:T(8,128)(2,1)S(1)}, u32[]{:S(2)}, u32[]{:S(2)}) collective-permute-start(bf16[2,64,128]{2,1,0:T(8,128)(2,1)S(1)} %get-tuple-element.32), channel_id=1, source_target_pairs={{5,0},{6,1},{7,2},{9,4},{10,5},{11,6},{13,8},{14,9},{15,10},{17,12... | collective-permute-start | bytes 98312 | tf_op jit(solution)/shard_map/ppermute | solution.py:77
  19.8 8.2 %collective-permute-start.2 = (bf16[2,2,64,128]{3,2,1,0:T(8,128)(2,1)S(1)}, bf16[2,2,64,128]{3,2,1,0:T(8,128)(2,1)S(1)}, u32[]{:S(2)}, u32[]{:S(2)}) collective-permute-start(bf16[2,2,64,128]{3,2,1,0:T(8,128)(2,1)S(1)} %get-tuple-element.27), channel_id=1, source_target_pairs={{0,1},{1,2},{2,3},{4,5},{5,6},{6,7},{8,9},{9,10},{10,11},{12,13},{... | collective-permute-start | bytes 196616 | tf_op jit(solution)/shard_map/ppermute | solution.py:66
  26.2 6.2 %collective-permute-start.3 = (bf16[2,2,64,128]{3,2,1,0:T(8,128)(2,1)S(1)}, bf16[2,2,64,128]{3,2,1,0:T(8,128)(2,1)S(1)}, u32[]{:S(2)}, u32[]{:S(2)}) collective-permute-start(bf16[2,2,64,128]{3,2,1,0:T(8,128)(2,1)S(1)} %get-tuple-element.28), channel_id=1, source_target_pairs={{1,0},{2,1},{3,2},{5,4},{6,5},{7,6},{9,8},{10,9},{11,10},{13,12},{... | collective-permute-start | bytes 196616 | tf_op jit(solution)/shard_map/ppermute | solution.py:67
  27.5 4.9 %copy-start.1 = (bf16[256,64]{0,1:T(8,128)(2,1)S(1)}, bf16[256,64]{0,1:T(8,128)(2,1)}, u32[]{:S(2)}) copy-start(bf16[256,64]{0,1:T(8,128)(2,1)} %param.8) | copy-start | bytes 98308
  27.5 4.9 %copy-start.2 = (bf16[64,256]{1,0:T(8,128)(2,1)S(1)}, bf16[64,256]{1,0:T(8,128)(2,1)}, u32[]{:S(2)}) copy-start(bf16[64,256]{1,0:T(8,128)(2,1)} %refs_13_.1) | copy-start | bytes 98308
  61.9 36.6 %all-to-all-start.1 = ((bf16[32,32,128]{2,1,0:T(8,128)(2,1)}), bf16[32,32,128]{2,1,0:T(8,128)(2,1)S(1)}, u32[]{:S(2)}, u32[]{:S(2)}) async-start(bf16[32,32,128]{2,1,0:T(8,128)(2,1)} %broadcast_in_dim.10), calls=%async_computation.1 | async-start | bytes 524288 | tf_op jit(solution)/shard_map/all_to_all | solution.py:353
  65.3 13.2 %collective-permute-start.9 = (bf16[1,1,256,128]{3,2,1,0:T(8,128)(2,1)S(1)}, bf16[1,1,256,128]{3,2,1,0:T(8,128)(2,1)S(1)}, u32[]{:S(2)}, u32[]{:S(2)}) collective-permute-start(bf16[1,1,256,128]{3,2,1,0:T(8,128)(2,1)S(1)} %constant_dynamic-slice_fusion), channel_id=1, source_target_pairs={{0,4},{4,0},{8,12},{12,8},{16,20},{20,16},{24,28},{28,24},{1,5},{5... | collective-permute-start | bytes 196616 | tf_op jit(solution)/shard_map/ppermute | solution.py:340
  65.6 15.1 %collective-permute-start.14 = (bf16[2,64,128]{2,1,0:T(8,128)(2,1)S(1)}, bf16[2,64,128]{2,1,0:T(8,128)(2,1)S(1)}, u32[]{:S(2)}, u32[]{:S(2)}) collective-permute-start(bf16[2,64,128]{2,1,0:T(8,128)(2,1)S(1)} %get-tuple-element.38), channel_id=1, source_target_pairs={{0,5},{1,6},{2,7},{4,9},{5,10},{6,11},{8,13},{9,14},{10,15},{12,17... | collective-permute-start | bytes 98312 | tf_op jit(solution)/shard_map/ppermute | solution.py:77
  68.9 13.1 %collective-permute-start.15 = (bf16[2,64,128]{2,1,0:T(8,128)(2,1)S(1)}, bf16[2,64,128]{2,1,0:T(8,128)(2,1)S(1)}, u32[]{:S(2)}, u32[]{:S(2)}) collective-permute-start(bf16[2,64,128]{2,1,0:T(8,128)(2,1)S(1)} %get-tuple-element.39), channel_id=1, source_target_pairs={{1,4},{2,5},{3,6},{5,8},{6,9},{7,10},{9,12},{10,13},{11,14},{13,16... | collective-permute-start | bytes 98312 | tf_op jit(solution)/shard_map/ppermute | solution.py:77
  70.2 18.2 %collective-permute-start.16 = (bf16[2,64,128]{2,1,0:T(8,128)(2,1)S(1)}, bf16[2,64,128]{2,1,0:T(8,128)(2,1)S(1)}, u32[]{:S(2)}, u32[]{:S(2)}) collective-permute-start(bf16[2,64,128]{2,1,0:T(8,128)(2,1)S(1)} %get-tuple-element.40), channel_id=1, source_target_pairs={{4,1},{5,2},{6,3},{8,5},{9,6},{10,7},{12,9},{13,10},{14,11},{16,13... | collective-permute-start | bytes 98312 | tf_op jit(solution)/shard_map/ppermute | solution.py:77
  76.3 18.3 %collective-permute-start.11 = (bf16[2,8,64,128]{3,2,1,0:T(8,128)(2,1)S(1)}, bf16[2,8,64,128]{3,2,1,0:T(8,128)(2,1)S(1)}, u32[]{:S(2)}, u32[]{:S(2)}) collective-permute-start(bf16[2,8,64,128]{3,2,1,0:T(8,128)(2,1)S(1)} %get-tuple-element.34.refs_0_), channel_id=1, source_target_pairs={{4,0},{8,4},{12,8},{16,12},{20,16},{24,20},{28,24},{5,1},{9,5},{13... | collective-permute-start | bytes 786440 | tf_op jit(solution)/shard_map/ppermute | solution.py:65
  78.5 16.1 %collective-permute-start.10 = (bf16[2,8,64,128]{3,2,1,0:T(8,128)(2,1)S(1)}, bf16[2,8,64,128]{3,2,1,0:T(8,128)(2,1)S(1)}, u32[]{:S(2)}, u32[]{:S(2)}) collective-permute-start(bf16[2,8,64,128]{3,2,1,0:T(8,128)(2,1)S(1)} %get-tuple-element.35.refs_1_), channel_id=1, source_target_pairs={{0,4},{4,8},{8,12},{12,16},{16,20},{20,24},{24,28},{1,5},{5,9},{9,... | collective-permute-start | bytes 786440 | tf_op jit(solution)/shard_map/ppermute | solution.py:64
  80.7 9.7 %collective-permute-start.17 = (bf16[2,64,128]{2,1,0:T(8,128)(2,1)S(1)}, bf16[2,64,128]{2,1,0:T(8,128)(2,1)S(1)}, u32[]{:S(2)}, u32[]{:S(2)}) collective-permute-start(bf16[2,64,128]{2,1,0:T(8,128)(2,1)S(1)} %get-tuple-element.41), channel_id=1, source_target_pairs={{5,0},{6,1},{7,2},{9,4},{10,5},{11,6},{13,8},{14,9},{15,10},{17,12... | collective-permute-start | bytes 98312 | tf_op jit(solution)/shard_map/ppermute | solution.py:77
  82.0 8.4 %collective-permute-start.12 = (bf16[2,2,64,128]{3,2,1,0:T(8,128)(2,1)S(1)}, bf16[2,2,64,128]{3,2,1,0:T(8,128)(2,1)S(1)}, u32[]{:S(2)}, u32[]{:S(2)}) collective-permute-start(bf16[2,2,64,128]{3,2,1,0:T(8,128)(2,1)S(1)} %get-tuple-element.36), channel_id=1, source_target_pairs={{0,1},{1,2},{2,3},{4,5},{5,6},{6,7},{8,9},{9,10},{10,11},{12,13},{... | collective-permute-start | bytes 196616 | tf_op jit(solution)/shard_map/ppermute | solution.py:66
  88.4 6.2 %collective-permute-start.13 = (bf16[2,2,64,128]{3,2,1,0:T(8,128)(2,1)S(1)}, bf16[2,2,64,128]{3,2,1,0:T(8,128)(2,1)S(1)}, u32[]{:S(2)}, u32[]{:S(2)}) collective-permute-start(bf16[2,2,64,128]{3,2,1,0:T(8,128)(2,1)S(1)} %get-tuple-element.37), channel_id=1, source_target_pairs={{1,0},{2,1},{3,2},{5,4},{6,5},{7,6},{9,8},{10,9},{11,10},{13,12},{... | collective-permute-start | bytes 196616 | tf_op jit(solution)/shard_map/ppermute | solution.py:67
